TPU v7x, 32 devices: a whole 2x2x4 slice. The times are simulated.
32 devices in a mesh: grp: 2 (over y), mem: 16 (over z, x, core).
Axes of the slice: x: 2, y: 2, z: 4, core: 2. Of those that a mesh axis runs over, the one named last changes fastest.
Arguments:
- user_factors: bfloat16 [32768, 256], P(('grp', 'mem')), may hold values from -1.5 to 1.5
- item_factors: bfloat16 [512, 256], P('mem'), may hold values from -1.5 to 1.5
- link_weights: bfloat16 [4096, 256], replicated, may hold values from -0.09375 to 0.09375
- item_feat: bfloat16 [16, 32, 4096], P('mem', 'grp'), may hold values from -6 to 6
- tile_values: bfloat16 [768, 128, 128], P(('grp', 'mem')), may hold values from -6 to 6
- tile_scale: float32 [768], P(('grp', 'mem')), may hold values from 0.25 to 2
- tile_place: int32 [768], P(('grp', 'mem')), may hold values from 0 to 31, as said below
- tile_count: int32 [32], P(('grp', 'mem')), may hold values from 1 to 24, as said below
- user_noise: bfloat16 [32768, 256], P(('grp', 'mem')), may hold values from -6 to 6
- item_noise: bfloat16 [16, 32, 256], P('mem', 'grp'), may hold values from -6 to 6
- link_noise: bfloat16 [4096, 256], P(('grp', 'mem')), may hold values from -6 to 6
Outputs:
- new_users: float32 [32768, 256], P(('grp', 'mem'))
- new_items: float32 [16, 32, 256], P('mem', 'grp')
- new_link: float32 [4096, 256], P(('grp', 'mem'))
Inputs may be any that keep to these rules, and one draw needn't show every extreme that they name: `tile_place`: within one device's 24 slots the places are distinct. `tile_count`: some device uses all 24 slots in every draw.
All inputs are finite; a program needn't handle non-finite values.
Results may differ from a plain program's by a relative error of at most 0.002.
Values may be sent and summed in bfloat16 or wider, within the bound.
A program may use at most 128 MiB of HBM per device.

v0:
```python
import jax
import jax.numpy as jnp
from jax import lax
from jax.sharding import PartitionSpec as P

rate_user = 0.004
prior_user = 0.5
rate_item = 0.002
prior_item = 0.2
rate_link = 0.002
prior_link = 0.5
noise_scale = 0.1


def per_device(
    user_factors,
    item_factors,
    link_weights,
    item_feat,
    tile_values,
    tile_scale,
    tile_place,
    tile_count,
    user_noise,
    item_noise,
    link_noise,
):
    tile_side = tile_values.shape[1]
    slot_total = tile_values.shape[0]
    rank_width = user_factors.shape[1]
    panel_rows = item_factors.shape[0]
    owned_items = item_feat.shape[1]
    members = lax.axis_size("mem")
    panels = lax.all_gather(item_factors, "mem", axis=0, tiled=True)
    item_tiles = panels.shape[0] // tile_side
    user_tiles = user_factors.shape[0] // tile_side
    live_count = tile_count[0]
    tile_rows = tile_place // item_tiles
    tile_cols = tile_place % item_tiles
    user_blocks = user_factors.reshape(user_tiles, tile_side, rank_width)
    item_blocks = panels.reshape(item_tiles, tile_side, rank_width)
    block_count = 4
    block_size = slot_total // block_count
    slots = jnp.arange(slot_total, dtype=jnp.int32)
    inputs = (
        tile_values.reshape(block_count, block_size, tile_side, tile_side),
        tile_scale.reshape(block_count, block_size),
        tile_rows.reshape(block_count, block_size),
        tile_cols.reshape(block_count, block_size),
        slots.reshape(block_count, block_size),
    )

    def advance(totals, block):
        user_total, item_total = totals
        values, scales, block_rows, block_cols, block_slots = block
        picked_users = jnp.take(user_blocks, block_rows, axis=0)
        picked_items = jnp.take(item_blocks, block_cols, axis=0)
        predicted = jnp.einsum(
            "tak,tbk->tab", picked_users, picked_items, preferred_element_type=jnp.float32
        )
        rating = scales[:, None, None] * values.astype(jnp.float32)
        valid = block_slots < live_count
        errors = jnp.where(valid[:, None, None], rating - predicted, 0.0).astype(jnp.bfloat16)
        user_terms = jnp.einsum(
            "tab,tbk->tak", errors, picked_items, preferred_element_type=jnp.float32
        )
        item_terms = jnp.einsum(
            "tab,tak->tbk", errors, picked_users, preferred_element_type=jnp.float32
        )
        user_total = user_total.at[block_rows].add(user_terms)
        item_total = item_total.at[block_cols].add(item_terms)
        return ((user_total, item_total), None)

    start_totals = (
        jnp.zeros((user_tiles, tile_side, rank_width), jnp.float32),
        jnp.zeros((item_tiles, tile_side, rank_width), jnp.float32),
    )
    (user_total, item_total), unused = lax.scan(advance, start_totals, inputs)
    old_users = user_factors.astype(jnp.float32)
    new_users = (
        old_users
        + rate_user * user_total.reshape(-1, rank_width)
        - prior_user * old_users
        + noise_scale * user_noise.astype(jnp.float32)
    )
    item_grad = item_total.reshape(members, panel_rows, rank_width)
    within = lax.psum_scatter(item_grad, "mem", scatter_dimension=0, tiled=True)
    item_sum = lax.psum_scatter(within, "grp", scatter_dimension=1, tiled=True)
    own_start = lax.axis_index("grp") * owned_items
    own_items = lax.dynamic_slice_in_dim(item_factors, own_start, owned_items, 0).astype(
        jnp.float32
    )
    features = item_feat[0]
    prior_mean = jnp.dot(features, link_weights, preferred_element_type=jnp.float32)
    resid = own_items - prior_mean
    resid_low = resid.astype(jnp.bfloat16)
    link_term = lax.dot_general(
        features, resid_low, (((0,), (0,)), ((), ())), preferred_element_type=jnp.float32
    )
    link_rows = link_noise.shape[0]
    link_start = (lax.axis_index("grp") * members + lax.axis_index("mem")) * link_rows
    link_total = lax.psum(link_term, ("grp", "mem"))
    link_mine = lax.dynamic_slice_in_dim(link_total, link_start, link_rows, 0)
    old_link = lax.dynamic_slice_in_dim(link_weights, link_start, link_rows, 0).astype(jnp.float32)
    new_link = (
        old_link
        + rate_link * link_mine
        - prior_link * old_link
        + noise_scale * link_noise.astype(jnp.float32)
    )
    new_items = (
        own_items
        + rate_item * item_sum[0]
        - prior_item * resid
        + noise_scale * item_noise[0].astype(jnp.float32)
    )
    return (new_users, new_items.reshape(1, owned_items, rank_width), new_link)


def solution(mesh):
    in_specs = (
        P(("grp", "mem"), None),
        P("mem", None),
        P(),
        P("mem", "grp", None),
        P(("grp", "mem"), None, None),
        P(("grp", "mem")),
        P(("grp", "mem")),
        P(("grp", "mem")),
        P(("grp", "mem"), None),
        P("mem", "grp", None),
        P(("grp", "mem"), None),
    )
    out_specs = (P(("grp", "mem"), None), P("mem", "grp", None), P(("grp", "mem"), None))
    return jax.shard_map(
        per_device, mesh=mesh, in_specs=in_specs, out_specs=out_specs, check_vma=False
    )
```

profile of v0, /device:TPU:0, one launch (start us, length us, event | category | flops | bytes accessed | tf_op | source)
XLA Modules:
  0.0 308.4 jit_solution(5301476545050638428)
XLA Ops:
  8.1 0.6 multiply_add_fusion
  8.6 0.7 and_select_fusion
  9.5 25.4 %all_gather.3 = bf16[512,256]{1,0:T(8,128)(2,1)} all-gather(bf16[32,256]{1,0:T(8,128)(2,1)} %param.14), channel_id=1, replica_groups=mesh['grp'=2,'mem'=16] {'mem'}, dimensions={0}, use_global_device_ids=true | all-gather | bytes 278528 | tf_op jit(solution)/shard_map/all_gather | solution.py:34
  34.9 1.3 reshape.128
  36.2 1.1 broadcast_in_dim.40
  37.3 60.0 %while.12 = (s32[]{:T(128)}, f32[8,128,256]{2,1,0:T(8,128)}, f32[4,128,256]{2,1,0:T(8,128)S(1)}, s32[4,6]{1,0:T(4,128)S(1)}, s32[4,6]{1,0:T(4,128)}, /*index=5*/...) while((s32[]{:T(128)}, f32[8,128,256]{2,1,0:T(8,128)}, ...), condition=%wide.region_3.4_spmd, body=%wide.region_0.3_spmd.sunk | while | flops 152668272 | bytes 14165449 | solution.py:78
  37.4 1.6 gather_fusion
  39.0 1.7 gather_fusion.1
  40.7 0.7 compare_and_fusion.3
  41.4 1.3 compare_bitcast_fusion.2
  42.7 0.7 fusion.33
  43.4 1.3 fusion.34
  44.7 0.7 copy-done.5
  45.4 1.3 fusion.35
  46.7 3.0 scatter_fusion
  49.7 1.4 fusion.36
  51.2 1.1 scatter_fusion.1
  52.4 1.6 gather_fusion
  54.0 1.7 gather_fusion.1
  55.7 0.7 compare_and_fusion.3
  56.4 1.3 compare_bitcast_fusion.2
  57.7 0.7 fusion.33
  58.4 1.3 fusion.34
  59.7 0.7 copy-done.5
  60.4 1.3 fusion.35
  61.7 3.0 scatter_fusion
  64.7 1.4 fusion.36
  66.2 1.1 scatter_fusion.1
  67.3 1.6 gather_fusion
  69.0 1.7 gather_fusion.1
  70.7 0.7 compare_and_fusion.3
  71.4 1.3 compare_bitcast_fusion.2
  72.7 0.7 fusion.33
  73.4 1.3 fusion.34
  74.7 0.7 copy-done.5
  75.4 1.3 fusion.35
  76.7 3.0 scatter_fusion
  79.7 1.4 fusion.36
  81.1 1.1 scatter_fusion.1
  82.3 1.6 gather_fusion
  84.0 1.7 gather_fusion.1
  85.7 0.7 compare_and_fusion.3
  86.4 1.3 compare_bitcast_fusion.2
  87.7 0.7 fusion.33
  88.4 1.3 fusion.34
  89.7 0.7 copy-done.5
  90.4 1.3 fusion.35
  91.7 3.0 scatter_fusion
  94.7 1.4 fusion.36
  96.2 1.1 scatter_fusion.1
  97.3 0.8 copy-done.1
  98.2 1.1 convolution_subtract_fusion.1
  99.3 52.1 %reduce-scatter.3.cloned.1.call-done = f32[1,32,256]{2,1,0:T(8,128)} async-done(((f32[16,32,256]{2,1,0:T(8,128)}), f32[1,32,256]{2,1,0:T(8,128)}) %reduce-scatter.3.cloned.1.call-update) | async-done | bytes 32784 | tf_op jit(solution)/shard_map/reduce_scatter | solution.py:87
  151.5 2.7 convolution_bitcast_fusion
  154.4 0.7 copy-done.10
  155.2 0.3 copy-done.4
  155.6 0.7 copy-done.6
  156.3 0.2 copy-done.8
  156.5 1.2 fusion.11
  157.7 4.9 %reduce-scatter.5.cloned.1.call-done = f32[1,16,256]{2,1,0:T(8,128)} async-done(((f32[1,32,256]{2,1,0:T(8,128)}), f32[1,16,256]{2,1,0:T(8,128)}) %reduce-scatter.5.cloned.1.call-update) | async-done | bytes 16400 | tf_op jit(solution)/shard_map/reduce_scatter | solution.py:88
  162.6 1.3 fusion.18
  163.9 135.3 %all-reduce.2.cloned.1.call-done = f32[4096,256]{0,1:T(8,128)} async-done(((f32[4096,256]{0,1:T(8,128)}), f32[4096,256]{0,1:T(8,128)}) %all-reduce.2.cloned.1.call-update) | async-done | bytes 4194320 | tf_op jit(solution)/shard_map/psum | solution.py:102
  299.2 0.9 fusion.13
  300.2 0.8 copy.17
  (74 shorter events, 0.9 us)
Async XLA Ops:
  8.0 90.2 %copy-start = (bf16[4096,256]{1,0:T(8,128)(2,1)S(1)}, bf16[4096,256]{1,0:T(8,128)(2,1)}, u32[]{:S(2)}) copy-start(bf16[4096,256]{1,0:T(8,128)(2,1)} %param.15) | copy-start | bytes 6291460
  8.0 143.4 %reduce-scatter.3.cloned.1.call-start = ((), (), s32[]{:S(2)}) async-start(), calls=%async_computation.2 | async-start | bytes 557056 | tf_op jit(solution)/shard_map/reduce_scatter | solution.py:87
  37.3 60.9 %copy-start.7 = (bf16[1,16,4096]{2,1,0:T(8,128)(2,1)S(1)}, bf16[1,16,4096]{2,1,0:T(8,128)(2,1)}, u32[]{:S(2)}) copy-start(bf16[1,16,4096]{2,1,0:T(8,128)(2,1)} %param.16) | copy-start | bytes 393220
  37.3 1.7 copy-start.11
  39.0 4.4 %copy-start.2 = (bf16[6,128,256]{2,1,0:T(8,128)(2,1)}, bf16[6,128,256]{2,1,0:T(8,128)(2,1)S(1)}, u32[]{:S(2)}) copy-start(bf16[6,128,256]{2,1,0:T(8,128)(2,1)S(1)} %gather_fusion) | copy-start | bytes 1179652 | tf_op jit(solution)/shard_map/while
  40.7 2.7 copy-start.3
  44.7 0.7 copy-start.5
  51.1 1.1 copy-start.12
  52.3 1.7 copy-start.11
  54.0 4.4 %copy-start.2 = (bf16[6,128,256]{2,1,0:T(8,128)(2,1)}, bf16[6,128,256]{2,1,0:T(8,128)(2,1)S(1)}, u32[]{:S(2)}) copy-start(bf16[6,128,256]{2,1,0:T(8,128)(2,1)S(1)} %gather_fusion) | copy-start | bytes 1179652 | tf_op jit(solution)/shard_map/while
  55.7 2.7 copy-start.3
  59.7 0.7 copy-start.5
  66.1 1.1 copy-start.12
  67.3 1.7 copy-start.11
  69.0 4.4 %copy-start.2 = (bf16[6,128,256]{2,1,0:T(8,128)(2,1)}, bf16[6,128,256]{2,1,0:T(8,128)(2,1)S(1)}, u32[]{:S(2)}) copy-start(bf16[6,128,256]{2,1,0:T(8,128)(2,1)S(1)} %gather_fusion) | copy-start | bytes 1179652 | tf_op jit(solution)/shard_map/while
  70.7 2.7 copy-start.3
  74.7 0.7 copy-start.5
  81.1 1.1 copy-start.12
  82.3 1.7 copy-start.11
  84.0 4.4 %copy-start.2 = (bf16[6,128,256]{2,1,0:T(8,128)(2,1)}, bf16[6,128,256]{2,1,0:T(8,128)(2,1)S(1)}, u32[]{:S(2)}) copy-start(bf16[6,128,256]{2,1,0:T(8,128)(2,1)S(1)} %gather_fusion) | copy-start | bytes 1179652 | tf_op jit(solution)/shard_map/while
  85.7 2.7 copy-start.3
  89.7 0.7 copy-start.5
  96.2 1.1 copy-start.12
  97.3 0.8 copy-start.1
  98.1 64.4 %reduce-scatter.5.cloned.1.call-start = ((), (), s32[]{:S(2)}) async-start(), calls=%async_computation.3 | async-start | bytes 49152 | tf_op jit(solution)/shard_map/reduce_scatter | solution.py:88
  151.5 147.8 %all-reduce.2.cloned.1.call-start = ((), (), s32[]{:S(2)}) async-start(), calls=%async_computation.4 | async-start | bytes 8388608 | tf_op jit(solution)/shard_map/psum | solution.py:102
  154.2 0.8 copy-start.10
  154.2 1.3 copy-start.4
  155.2 1.1 copy-start.6
  155.2 1.3 copy-start.8
  156.5 6.1 %copy-start.9 = (bf16[32,256]{1,0:T(8,128)(2,1)S(1)}, bf16[32,256]{1,0:T(8,128)(2,1)}, u32[]{:S(2)}) copy-start(bf16[32,256]{1,0:T(8,128)(2,1)} %param.14) | copy-start | bytes 49156
  156.5 6.1 %copy-start.13 = (bf16[1,16,256]{2,1,0:T(8,128)(2,1)S(1)}, bf16[1,16,256]{2,1,0:T(8,128)(2,1)}, u32[]{:S(2)}) copy-start(bf16[1,16,256]{2,1,0:T(8,128)(2,1)} %param.22) | copy-start | bytes 24580
Sparse Core Ops, SparseCore 0:
  98.3 53.1 reduce-scatter.2
  153.7 8.8 reduce-scatter.4
Sparse Core Ops, SparseCore 1:
  158.4 140.8 all-reduce.1
where the time goes:
time: 310 us; the launch traced here: 308 us
  waiting for transfers between devices  192 us (62%)
  other arithmetic  29.5 us (10%)
  blocking collectives  25.4 us (8%)
  local copies, waits for them, and re-layouts  24.8 us (8%)
  matrix products  19.9 us (6%)
  between operations  15.6 us (5%)
    psum x1, waiting for transfers between devices, per_device(): link_total = lax.psum(link_term, ('grp', 'mem'))  135 us
    reduce_scatter x1, waiting for transfers between devices, per_device(): within = lax.psum_scatter(item_grad, 'mem', scatter_dimension=0, tiled=True)  52.1 us
    all_gather x1, blocking collectives, per_device(): panels = lax.all_gather(item_factors, 'mem', axis=0, tiled=True)  25.4 us
    scatter-add x4, other arithmetic, advance(): user_total = user_total.at[block_rows].add(user_terms)  12.1 us
    gather x4, local copies, waits for them, and re-layouts, advance(): picked_items = jnp.take(item_blocks, block_cols, axis=0)  6.64 us
    gather x4, local copies, waits for them, and re-layouts, advance(): picked_users = jnp.take(user_blocks, block_rows, axis=0)  6.46 us
  transfers between devices with their start and end apart: 3, of which 3 were waited for; matrix products, arithmetic and copies ran while one was open for 2% of the time, Pallas kernels for 0%

commit v1 on v0

v1 whole, which is shorter than its diff:
```python
import functools

import jax
import jax.numpy as jnp
from jax import lax
from jax.experimental import pallas as pl
from jax.experimental.pallas import tpu as pltpu
from jax.sharding import PartitionSpec as P

rate_user = 0.004
prior_user = 0.5
rate_item = 0.002
prior_item = 0.2
rate_link = 0.002
prior_link = 0.5
noise_scale = 0.1

f32 = jnp.float32
bf16 = jnp.bfloat16
MESH = pl.DeviceIdType.MESH


def kernel(
    groups,
    members,
    slot_of,
    scales,
    panel,
    feats,
    cut,
    item_noise,
    link_noise,
    users_hbm,
    weights_hbm,
    tiles_hbm,
    noise_hbm,
    new_users,
    new_items,
    new_link,
    users,
    weights,
    tiles,
    noise,
    items,
    feat_all,
    resid_all,
    grad_send,
    grad_all,
    errors,
    user_sum,
    local_sem,
    send_sem,
    recv_sem,
):
    n = groups * members
    grp = lax.axis_index("grp")
    mem = lax.axis_index("mem")
    me = grp * members + mem
    own = mem * groups + grp
    panel_rows, rank = panel.shape
    owned = feats.shape[0]
    link_rows = link_noise.shape[0]
    side = tiles.shape[1]
    user_tiles = users.shape[0] // side
    item_tiles = items.shape[0] * panel_rows // side

    loads = [
        pltpu.make_async_copy(weights_hbm, weights, local_sem.at[0]),
        pltpu.make_async_copy(users_hbm, users, local_sem.at[1]),
        pltpu.make_async_copy(tiles_hbm, tiles, local_sem.at[2]),
        pltpu.make_async_copy(noise_hbm, noise, local_sem.at[3]),
    ]
    for load in loads:
        load.start()

    def place(d):
        return {"grp": d // members, "mem": lax.rem(d, members)}

    barrier = pltpu.get_barrier_semaphore()

    def greet(k, carry):
        d = lax.rem(me + k, n)
        pl.semaphore_signal(barrier, inc=1, device_id=place(d), device_id_type=MESH)
        return carry

    lax.fori_loop(1, n, greet, 0)
    items[mem] = panel[...]
    if cut is None:
        feat_all[me] = feats[:, pl.ds(pl.multiple_of(me * link_rows, link_rows), link_rows)]
    else:
        feat_all[me] = cut[me]
    pl.semaphore_wait(barrier, n - 1)

    def send_panel(k, carry):
        m = lax.rem(mem + k, members)
        pltpu.make_async_remote_copy(
            src_ref=panel,
            dst_ref=items.at[mem],
            send_sem=send_sem.at[0],
            recv_sem=recv_sem.at[0],
            device_id={"grp": grp, "mem": m},
            device_id_type=MESH,
        ).start()
        return carry

    lax.fori_loop(1, members, send_panel, 0)

    def send_feat(k, carry):
        d = lax.rem(me + k, n)
        if cut is None:
            source = feats.at[:, pl.ds(pl.multiple_of(d * link_rows, link_rows), link_rows)]
        else:
            source = cut.at[d]
        pltpu.make_async_remote_copy(
            src_ref=source,
            dst_ref=feat_all.at[me],
            send_sem=send_sem.at[1],
            recv_sem=recv_sem.at[1],
            device_id=place(d),
            device_id_type=MESH,
        ).start()
        return carry

    lax.fori_loop(1, n, send_feat, 0)

    loads[0].wait()
    start = pl.multiple_of(grp * owned, owned)
    own_items = panel[pl.ds(start, owned), :].astype(f32)
    resid = own_items - jnp.dot(feats[...], weights[...], preferred_element_type=f32)
    resid_all[me] = resid.astype(bf16)

    def send_resid(k, carry):
        d = lax.rem(me + k, n)
        pltpu.make_async_remote_copy(
            src_ref=resid_all.at[me],
            dst_ref=resid_all.at[me],
            send_sem=send_sem.at[2],
            recv_sem=recv_sem.at[2],
            device_id=place(d),
            device_id_type=MESH,
        ).start()
        return carry

    lax.fori_loop(1, n, send_resid, 0)

    def wait_all(buffer, count, sem):
        part = buffer.at[pl.ds(0, count)]
        pltpu.make_async_copy(part, part, sem).wait()

    loads[1].wait()
    loads[2].wait()
    wait_all(items, members - 1, recv_sem.at[0])

    wide = 2 if item_tiles % 2 == 0 else 1
    tall = 2 if user_tiles % 2 == 0 else 1
    chunk = wide * side
    panels_in = chunk // panel_rows
    owners_in = chunk // owned

    def do_chunk(c, first):
        block = items[pl.ds(c * panels_in, panels_in)].reshape(chunk, rank)
        for t in range(user_tiles // tall):
            rows = pl.ds(t * tall * side, tall * side)
            predicted = lax.dot_general(
                users[rows, :], block, (((1,), (1,)), ((), ())), preferred_element_type=f32
            )
            for a in range(tall):
                for b in range(wide):
                    slot = slot_of[(t * tall + a) * item_tiles + c * wide + b]
                    at = jnp.maximum(slot, 0)
                    live = (slot >= 0).astype(f32)
                    rating = scales[at] * tiles[at].astype(f32)
                    part = predicted[a * side : (a + 1) * side, b * side : (b + 1) * side]
                    errors[pl.ds((t * tall + a) * side, side), b * side : (b + 1) * side] = (
                        (rating - part) * live
                    ).astype(bf16)
            term = jnp.dot(errors[rows, :], block, preferred_element_type=f32)
            if first:
                user_sum[rows, :] = term
            else:
                user_sum[rows, :] += term
        grads = lax.dot_general(
            errors[...], users[...], (((0,), (0,)), ((), ())), preferred_element_type=f32
        )
        grad_send[pl.ds(c * owners_in, owners_in)] = grads.astype(bf16).reshape(
            owners_in, owned, rank
        )

        def send_grad(j, carry):
            o = c * owners_in + j

            @pl.when(o != own)
            def _():
                pltpu.make_async_remote_copy(
                    src_ref=grad_send.at[o],
                    dst_ref=grad_all.at[me],
                    send_sem=send_sem.at[3],
                    recv_sem=recv_sem.at[3],
                    device_id={"grp": lax.rem(o, groups), "mem": o // groups},
                    device_id_type=MESH,
                ).start()

            return carry

        lax.fori_loop(0, owners_in, send_grad, 0)

    chunks = item_tiles // wide
    if chunks <= 4:
        for c in range(chunks):
            do_chunk(c, c == 0)
    else:
        do_chunk(0, True)

        def later(c, carry):
            do_chunk(c, False)
            return carry

        lax.fori_loop(1, chunks, later, 0)

    loads[3].wait()
    for t in range(user_tiles):
        rows = pl.ds(t * side, side)
        user_sum[rows, :] = (
            (1.0 - prior_user) * users[rows, :].astype(f32)
            + rate_user * user_sum[rows, :]
            + noise_scale * noise[rows, :].astype(f32)
        )
    store = pltpu.make_async_copy(user_sum, new_users, local_sem.at[4])
    store.start()

    wait_all(feat_all, n - 1, recv_sem.at[1])
    wait_all(resid_all, n - 1, recv_sem.at[2])
    link_sum = lax.dot_general(
        feat_all[...].reshape(n * owned, link_rows),
        resid_all[...].reshape(n * owned, rank),
        (((0,), (0,)), ((), ())),
        preferred_element_type=f32,
    )
    old_link = weights[pl.ds(pl.multiple_of(me * link_rows, link_rows), link_rows), :].astype(f32)
    new_link[...] = (
        (1.0 - prior_link) * old_link
        + rate_link * link_sum
        + noise_scale * link_noise[...].astype(f32)
    )

    grad_all[me] = grad_send[own]
    wait_all(grad_all, n - 1, recv_sem.at[3])

    def gather(k, total):
        return total + jnp.sum(grad_all[pl.ds(k * 8, 8)].astype(f32), axis=0)

    item_sum = lax.fori_loop(0, n // 8, gather, jnp.zeros((owned, rank), f32))
    new_items[...] = (
        own_items
        + rate_item * item_sum
        - prior_item * resid
        + noise_scale * item_noise[...].astype(f32)
    )

    wait_all(items, members - 1, send_sem.at[0])
    wait_all(feat_all, n - 1, send_sem.at[1])
    wait_all(resid_all, n - 1, send_sem.at[2])
    wait_all(grad_all, n - 1, send_sem.at[3])
    store.wait()


def narrow_kernel(groups, members, *refs):
    kernel(groups, members, *refs[:4], None, *refs[4:])


def per_device(
    user_factors,
    item_factors,
    link_weights,
    item_feat,
    tile_values,
    tile_scale,
    tile_place,
    tile_count,
    user_noise,
    item_noise,
    link_noise,
):
    groups = lax.axis_size("grp")
    members = lax.axis_size("mem")
    n = groups * members
    slots, side, unused = tile_values.shape
    user_count, rank = user_factors.shape
    panel_rows = item_factors.shape[0]
    owned = item_feat.shape[1]
    features = item_feat.shape[2]
    link_rows = link_noise.shape[0]
    places = (user_count // side) * (panel_rows * members // side)
    numbers = jnp.arange(slots, dtype=jnp.int32)
    match = (tile_place[None, :] == jnp.arange(places, dtype=jnp.int32)[:, None]) & (
        numbers < tile_count[0]
    )[None, :]
    slot_of = jnp.max(jnp.where(match, numbers[None, :], -1), axis=1)
    feats = item_feat[0]

    smem = pl.BlockSpec(memory_space=pltpu.SMEM)
    vmem = pl.BlockSpec(memory_space=pltpu.VMEM)
    hbm = pl.BlockSpec(memory_space=pl.ANY)
    operands = [slot_of, tile_scale, item_factors, feats]
    specs = [smem, smem, vmem, vmem]
    if link_rows % 128:
        operands.append(feats.reshape(owned, n, link_rows).transpose(1, 0, 2))
        specs.append(vmem)
        body = functools.partial(kernel, groups, members)
    else:
        body = functools.partial(narrow_kernel, groups, members)
    operands += [item_noise[0], link_noise, user_factors, link_weights, tile_values, user_noise]
    specs += [vmem, vmem, hbm, hbm, hbm, hbm]
    chunk = 2 * side if (panel_rows * members // side) % 2 == 0 else side
    new_users, new_items, new_link = pl.pallas_call(
        body,
        out_shape=(
            jax.ShapeDtypeStruct((user_count, rank), f32),
            jax.ShapeDtypeStruct((owned, rank), f32),
            jax.ShapeDtypeStruct((link_rows, rank), f32),
        ),
        in_specs=specs,
        out_specs=(hbm, vmem, vmem),
        scratch_shapes=[
            pltpu.VMEM((user_count, rank), bf16),
            pltpu.VMEM((features, rank), bf16),
            pltpu.VMEM((slots, side, side), bf16),
            pltpu.VMEM((user_count, rank), bf16),
            pltpu.VMEM((members, panel_rows, rank), bf16),
            pltpu.VMEM((n, owned, link_rows), bf16),
            pltpu.VMEM((n, owned, rank), bf16),
            pltpu.VMEM((n, owned, rank), bf16),
            pltpu.VMEM((n, owned, rank), bf16),
            pltpu.VMEM((user_count, chunk), bf16),
            pltpu.VMEM((user_count, rank), f32),
            pltpu.SemaphoreType.DMA((5,)),
            pltpu.SemaphoreType.DMA((4,)),
            pltpu.SemaphoreType.DMA((4,)),
        ],
        compiler_params=pltpu.CompilerParams(
            collective_id=0, has_side_effects=True, vmem_limit_bytes=48 * 1024 * 1024
        ),
    )(*operands)
    return (new_users, new_items[None], new_link)


def solution(mesh):
    in_specs = (
        P(("grp", "mem"), None),
        P("mem", None),
        P(),
        P("mem", "grp", None),
        P(("grp", "mem"), None, None),
        P(("grp", "mem")),
        P(("grp", "mem")),
        P(("grp", "mem")),
        P(("grp", "mem"), None),
        P("mem", "grp", None),
        P(("grp", "mem"), None),
    )
    out_specs = (P(("grp", "mem"), None), P("mem", "grp", None), P(("grp", "mem"), None))
    return jax.shard_map(
        per_device, mesh=mesh, in_specs=in_specs, out_specs=out_specs, check_vma=False
    )
```

time: 310 us -> 40.7 us (0.13)
  waiting for transfers between devices: 192 us -> 0 us
  other arithmetic: 29.5 us -> 0.75 us
  Pallas kernels: 0 us -> 27.3 us
  blocking collectives: 25.4 us -> 0 us
  matrix products: 19.9 us -> 0 us
  between operations: 15.6 us -> 1.31 us
  local copies, waits for them, and re-layouts: 24.8 us -> 10.8 us
    psum x1 -> x0, waiting for transfers between devices: 135 us -> none  [per_device(): link_total = lax.psum(link_term, ('grp', 'mem'))]
    reduce_scatter x2 -> x0, waiting for transfers between devices: 57.1 us -> none  [the longest x1 52.1 us: per_device(): within = lax.psum_scatter(item_grad, 'mem', scatter_dimension=0, tiled=True)]
    pallas_call x0 -> x1, Pallas kernels: none -> 27.3 us  [per_device(): pl.pallas_call(body, out_shape=(jax.ShapeDtypeStruct((user_count, rank),...]
    all_gather x1 -> x0, blocking collectives: 25.4 us -> none  [per_device(): panels = lax.all_gather(item_factors, 'mem', axis=0, tiled=True)]
    dot_general x14 -> x0, matrix products: 19.9 us -> none  [the longest x4 5.72 us: advance(): jnp.einsum('tab,tak->tbk', errors, picked_users, preferred_element_type=j...]
    scatter-add x8 -> x0, other arithmetic: 16.5 us -> none  [the longest x4 12.1 us: advance(): user_total = user_total.at[block_rows].add(user_terms)]
    gather x8 -> x0, local copies, waits for them, and re-layouts: 13.1 us -> none  [the longest x4 6.64 us: advance(): picked_items = jnp.take(item_blocks, block_cols, axis=0)]
    unnamed x21, local copies, waits for them, and re-layouts: 3.63 us -> 10.8 us
  transfers between devices with their start and end apart: 3 -> 0, of which waited for: 3 -> 0; matrix products, arithmetic and copies ran while one was open for 2% -> 0% of each run, Pallas kernels for 0% -> 0%
where the time goes in v1:
time: 40.7 us; the launch traced here: 40.3 us
  Pallas kernels  27.3 us (67%)
  local copies, waits for them, and re-layouts  10.8 us (27%)
  between operations  1.31 us (3%)
  other arithmetic  0.75 us (2%)
    pallas_call x1, Pallas kernels, per_device(): pl.pallas_call(body, out_shape=(jax.ShapeDtypeStruct((user_count, rank),...  27.3 us
    unnamed x21, local copies, waits for them, and re-layouts  10.8 us

profile of v1, /device:TPU:0, one launch (start us, length us, event | category | flops | bytes accessed | tf_op | source)
XLA Modules:
  0.0 40.3 jit_solution(15692765481268865350)
XLA Ops:
  1.3 0.7 %select_reduce_fusion.refs_0_ = s32[32]{0:T(128)S(1)} fusion(s32[24]{0:T(128)} %param.17, pred[24]{0:T(512)(128)(4,1)S(1)} %iota_compare_fusion.1), kind=kLoop, calls=%fused_computation | loop fusion | flops 3040 | bytes 248 | tf_op jit(solution)/shard_map/reduce_max | solution.py:298
  2.0 0.0 copy-start
  2.0 1.6 %copy-done = bf16[4096,256]{1,0:T(8,128)(2,1)S(1)} copy-done((bf16[4096,256]{1,0:T(8,128)(2,1)S(1)}, bf16[4096,256]{1,0:T(8,128)(2,1)}, u32[]{:S(2)}) %copy-start) | copy-done | bytes 2097176
  3.6 0.0 copy-start.1
  3.6 1.1 %copy-done.1 = bf16[24,128,128]{2,1,0:T(8,128)(2,1)S(1)} copy-done((bf16[24,128,128]{2,1,0:T(8,128)(2,1)S(1)}, bf16[24,128,128]{2,1,0:T(8,128)(2,1)}, u32[]{:S(2)}) %copy-start.1) | copy-done | bytes 786456
  4.8 0.0 copy-start.2
  4.8 1.0 %copy-done.2 = bf16[1024,256]{1,0:T(8,128)(2,1)S(1)} copy-done((bf16[1024,256]{1,0:T(8,128)(2,1)S(1)}, bf16[1024,256]{1,0:T(8,128)(2,1)}, u32[]{:S(2)}) %copy-start.2) | copy-done | bytes 524312
  5.8 0.0 copy-start.3
  5.8 1.0 %copy-done.3 = bf16[1024,256]{1,0:T(8,128)(2,1)S(1)} copy-done((bf16[1024,256]{1,0:T(8,128)(2,1)S(1)}, bf16[1024,256]{1,0:T(8,128)(2,1)}, u32[]{:S(2)}) %copy-start.3) | copy-done | bytes 524312
  6.8 0.0 copy-start.4
  6.8 0.9 %copy-done.4 = bf16[1,16,4096]{2,1,0:T(8,128)(2,1)S(1)} copy-done((bf16[1,16,4096]{2,1,0:T(8,128)(2,1)S(1)}, bf16[1,16,4096]{2,1,0:T(8,128)(2,1)}, u32[]{:S(2)}) %copy-start.4) | copy-done | bytes 131096
  7.8 0.0 copy-start.5
  7.8 0.8 %copy-done.5 = bf16[128,256]{1,0:T(8,128)(2,1)S(1)} copy-done((bf16[128,256]{1,0:T(8,128)(2,1)S(1)}, bf16[128,256]{1,0:T(8,128)(2,1)}, u32[]{:S(2)}) %copy-start.5) | copy-done | bytes 65560
  8.6 0.0 copy-start.6
  8.6 0.7 %copy-done.6 = bf16[32,256]{1,0:T(8,128)(2,1)S(1)} copy-done((bf16[32,256]{1,0:T(8,128)(2,1)S(1)}, bf16[32,256]{1,0:T(8,128)(2,1)}, u32[]{:S(2)}) %copy-start.6) | copy-done | bytes 16408
  9.3 0.0 copy-start.7
  9.3 0.7 %copy-done.7 = bf16[1,16,256]{2,1,0:T(8,128)(2,1)S(1)} copy-done((bf16[1,16,256]{2,1,0:T(8,128)(2,1)S(1)}, bf16[1,16,256]{2,1,0:T(8,128)(2,1)}, u32[]{:S(2)}) %copy-start.7) | copy-done | bytes 8216
  10.0 0.0 copy-start.8
  10.0 0.7 %copy-done.8 = f32[24]{0:T(128)S(1)} copy-done((f32[24]{0:T(128)S(1)}, f32[24]{0:T(128)}, u32[]{:S(2)}) %copy-start.8) | copy-done | bytes 120
  10.7 27.3 %shard_map.130 = (f32[1024,256]{1,0:T(8,128)S(1)}, f32[16,256]{1,0:T(8,128)S(1)}, f32[128,256]{1,0:T(8,128)S(1)}) custom-call(s32[32]{0:T(128)S(1)} %select_reduce_fusion.refs_0_, f32[24]{0:T(128)S(1)} %copy-done.8, bf16[32,256]{1,0:T(8,128)(2,1)S(1)} %copy-done.6, bf16[16,4096]{1,0:T(8,128)(2,1)S(1)} %bitcast.5, bf16[16,256]{1,0:T(8,128)(2,1)S(1)} %bitcast.7, ...), custom_call_target="tpu_custom_call" | custom-call | tf_op jit(solution)/shard_map/pallas_call | solution.py:315
  38.0 1.0 %copy.18 = f32[1024,256]{1,0:T(8,128)} copy(f32[1024,256]{1,0:T(8,128)S(1)} %get-tuple-element.12) | data formatting | bytes 2097152
  39.0 0.6 %copy.19 = f32[1,16,256]{2,1,0:T(8,128)} copy(f32[1,16,256]{2,1,0:T(8,128)S(1)} %bitcast.6) | data formatting | bytes 32768
  39.6 0.7 %copy.20 = f32[128,256]{1,0:T(8,128)} copy(f32[128,256]{1,0:T(8,128)S(1)} %get-tuple-element.14) | data formatting | bytes 262144
  (1 shorter events, 0.0 us)
Async XLA Ops:
  2.0 1.6 %copy-start = (bf16[4096,256]{1,0:T(8,128)(2,1)S(1)}, bf16[4096,256]{1,0:T(8,128)(2,1)}, u32[]{:S(2)}) copy-start(bf16[4096,256]{1,0:T(8,128)(2,1)} %refs_7_.1) | copy-start | bytes 6291460
  3.6 1.1 %copy-start.1 = (bf16[24,128,128]{2,1,0:T(8,128)(2,1)S(1)}, bf16[24,128,128]{2,1,0:T(8,128)(2,1)}, u32[]{:S(2)}) copy-start(bf16[24,128,128]{2,1,0:T(8,128)(2,1)} %refs_8_.1) | copy-start | bytes 2359300
  4.8 1.0 %copy-start.2 = (bf16[1024,256]{1,0:T(8,128)(2,1)S(1)}, bf16[1024,256]{1,0:T(8,128)(2,1)}, u32[]{:S(2)}) copy-start(bf16[1024,256]{1,0:T(8,128)(2,1)} %refs_6_.1) | copy-start | bytes 1572868
  5.8 1.0 %copy-start.3 = (bf16[1024,256]{1,0:T(8,128)(2,1)S(1)}, bf16[1024,256]{1,0:T(8,128)(2,1)}, u32[]{:S(2)}) copy-start(bf16[1024,256]{1,0:T(8,128)(2,1)} %refs_9_.1) | copy-start | bytes 1572868
  6.8 0.9 %copy-start.4 = (bf16[1,16,4096]{2,1,0:T(8,128)(2,1)S(1)}, bf16[1,16,4096]{2,1,0:T(8,128)(2,1)}, u32[]{:S(2)}) copy-start(bf16[1,16,4096]{2,1,0:T(8,128)(2,1)} %param.14) | copy-start | bytes 393220
  7.8 0.8 %copy-start.5 = (bf16[128,256]{1,0:T(8,128)(2,1)S(1)}, bf16[128,256]{1,0:T(8,128)(2,1)}, u32[]{:S(2)}) copy-start(bf16[128,256]{1,0:T(8,128)(2,1)} %refs_5_.1) | copy-start | bytes 196612
  8.6 0.7 %copy-start.6 = (bf16[32,256]{1,0:T(8,128)(2,1)S(1)}, bf16[32,256]{1,0:T(8,128)(2,1)}, u32[]{:S(2)}) copy-start(bf16[32,256]{1,0:T(8,128)(2,1)} %refs_2_.1) | copy-start | bytes 49156
  9.3 0.7 %copy-start.7 = (bf16[1,16,256]{2,1,0:T(8,128)(2,1)S(1)}, bf16[1,16,256]{2,1,0:T(8,128)(2,1)}, u32[]{:S(2)}) copy-start(bf16[1,16,256]{2,1,0:T(8,128)(2,1)} %param.20) | copy-start | bytes 24580
  10.0 0.7 %copy-start.8 = (f32[24]{0:T(128)S(1)}, f32[24]{0:T(128)}, u32[]{:S(2)}) copy-start(f32[24]{0:T(128)} %refs_1_.1) | copy-start | bytes 292

commit v2 on v1

v2 whole, which is shorter than its diff:
```python
import functools

import jax
import jax.numpy as jnp
from jax import lax
from jax.experimental import pallas as pl
from jax.experimental.pallas import tpu as pltpu
from jax.sharding import PartitionSpec as P

rate_user = 0.004
prior_user = 0.5
rate_item = 0.002
prior_item = 0.2
rate_link = 0.002
prior_link = 0.5
noise_scale = 0.1

f32 = jnp.float32
bf16 = jnp.bfloat16
MESH = pl.DeviceIdType.MESH
VMEM_BYTES = 60 * 1024 * 1024


def kernel(
    groups,
    members,
    wide_cut,
    slot_of,
    scales,
    panel_hbm,
    cut_hbm,
    item_noise_hbm,
    link_noise_hbm,
    feats_hbm,
    users_hbm,
    weights_hbm,
    tiles_hbm,
    noise_hbm,
    new_users,
    new_items,
    new_link,
    panel,
    cut,
    item_noise,
    link_noise,
    feats,
    users,
    weights,
    tiles,
    noise,
    items,
    feat_out,
    feat_pair,
    feat_all,
    resid_all,
    grad_part,
    grad_in,
    grad_send,
    grad_all,
    errors,
    user_sum,
    item_out,
    link_out,
    local_sem,
    send_sem,
    recv_sem,
    part_sem,
):
    n = groups * members
    ring = members // 2
    chips = n // 2
    grp = lax.axis_index("grp")
    mem = lax.axis_index("mem")
    core = lax.rem(mem, 2)
    other = 1 - core
    spot = mem // 2
    chip = grp * ring + spot
    me = grp * members + mem
    panel_rows, rank = panel.shape
    owned = feats.shape[0]
    link_rows = link_noise.shape[0]
    side = tiles.shape[1]
    user_tiles = users.shape[0] // side
    item_tiles = members * panel_rows // side
    sibling = {"grp": grp, "mem": spot * 2 + other}

    def load(source, target, k):
        return pltpu.make_async_copy(source, target, local_sem.at[k])

    loads = [
        load(panel_hbm, panel, 0),
        load(feats_hbm, feats, 1),
        load(weights_hbm, weights, 2),
        None if wide_cut else load(cut_hbm, cut, 3),
        load(users_hbm, users, 4),
        load(tiles_hbm, tiles, 5),
        load(noise_hbm, noise, 6),
        load(link_noise_hbm, link_noise, 7),
        load(item_noise_hbm, item_noise, 8),
    ]
    for one in loads:
        if one is not None:
            one.start()

    def mate(q):
        return {"grp": q // ring, "mem": lax.rem(q, ring) * 2 + core}

    def send(source, target, k, device):
        pltpu.make_async_remote_copy(
            src_ref=source,
            dst_ref=target,
            send_sem=send_sem.at[k],
            recv_sem=recv_sem.at[k],
            device_id=device,
            device_id_type=MESH,
        ).start()

    def wait_for(part, sem):
        pltpu.make_async_copy(part, part, sem).wait()

    barrier = pltpu.get_barrier_semaphore()
    pl.semaphore_signal(barrier, inc=1, device_id=sibling, device_id_type=MESH)

    def greet(k, carry):
        q = lax.rem(chip + k, chips)
        pl.semaphore_signal(barrier, inc=1, device_id=mate(q), device_id_type=MESH)
        return carry

    lax.fori_loop(1, chips, greet, 0)

    loads[0].wait()
    items[spot, core] = panel[...]
    loads[1].wait()
    if not wide_cut:
        loads[3].wait()

    def piece(d):
        if wide_cut:
            return feats[:, pl.ds(pl.multiple_of(d * link_rows, link_rows), link_rows)]
        return cut[d]

    def pack(q, carry):
        feat_pair[q, core] = piece(q * 2 + core)
        feat_out[q] = piece(q * 2 + other)
        return carry

    lax.fori_loop(0, chips, pack, 0)
    pl.semaphore_wait(barrier, chips)

    def send_panel(k, carry):
        q = lax.rem(spot + k, ring)
        send(panel, items.at[spot, core], 0, {"grp": grp, "mem": q * 2 + core})
        return carry

    lax.fori_loop(1, ring, send_panel, 0)
    send(feat_out, feat_pair.at[:, core], 1, sibling)

    loads[2].wait()
    start = pl.multiple_of(grp * owned, owned)
    own_items = panel[pl.ds(start, owned), :].astype(f32)
    resid = own_items - jnp.dot(feats[...], weights[...], preferred_element_type=f32)
    resid_all[chip, core] = resid.astype(bf16)

    def send_resid(k, carry):
        q = lax.rem(chip + k, chips)
        send(resid_all.at[chip, core], resid_all.at[chip, core], 2, mate(q))
        return carry

    lax.fori_loop(1, chips, send_resid, 0)

    wait_for(items.at[pl.ds(0, ring - 1), 0], recv_sem.at[0])
    send(items.at[:, core], items.at[:, core], 3, sibling)

    wait_for(feat_out, recv_sem.at[1])
    feat_all[chip] = feat_pair[chip]

    def send_feat(k, carry):
        q = lax.rem(chip + k, chips)
        send(feat_pair.at[q], feat_all.at[chip], 4, mate(q))
        return carry

    lax.fori_loop(1, chips, send_feat, 0)

    loads[4].wait()
    loads[5].wait()
    wait_for(items.at[:, other], recv_sem.at[3])

    wide = 2
    tall = 2 if user_tiles % 2 == 0 else 1
    chunk = wide * side
    spots_in = chunk // panel_rows // 2

    def do_chunk(c, first):
        block = items[pl.ds(c * spots_in, spots_in)].reshape(chunk, rank)
        for t in range(user_tiles // tall):
            rows = pl.ds(t * tall * side, tall * side)
            predicted = lax.dot_general(
                users[rows, :], block, (((1,), (1,)), ((), ())), preferred_element_type=f32
            )
            for a in range(tall):
                for b in range(wide):
                    slot = slot_of[(t * tall + a) * item_tiles + c * wide + b]
                    at = jnp.maximum(slot, 0)
                    live = (slot >= 0).astype(f32)
                    rating = scales[at] * tiles[at].astype(f32)
                    part = predicted[a * side : (a + 1) * side, b * side : (b + 1) * side]
                    errors[pl.ds((t * tall + a) * side, side), b * side : (b + 1) * side] = (
                        (rating - part) * live
                    ).astype(bf16)
            term = jnp.dot(errors[rows, :], block, preferred_element_type=f32)
            if first:
                user_sum[rows, :] = term
            else:
                user_sum[rows, :] += term
        grads = lax.dot_general(
            errors[...], users[...], (((0,), (0,)), ((), ())), preferred_element_type=f32
        )
        span = pl.ds(c * spots_in, spots_in)
        grad_part[span] = grads.reshape(spots_in, 2, groups, owned, rank)
        pltpu.make_async_remote_copy(
            src_ref=grad_part.at[span, other],
            dst_ref=grad_in.at[span],
            send_sem=send_sem.at[5],
            recv_sem=part_sem.at[c],
            device_id=sibling,
            device_id_type=MESH,
        ).start()

    def finish(c):
        span = pl.ds(c * spots_in, spots_in)
        wait_for(grad_in.at[span], part_sem.at[c])
        grad_send[span] = (grad_part[span, core] + grad_in[span]).astype(bf16)

        def send_grad(j, carry):
            at = lax.rem(j + chip, spots_in * groups)
            to = c * spots_in + at // groups
            g = lax.rem(at, groups)

            @pl.when(g * ring + to != chip)
            def _():
                send(
                    grad_send.at[to, g],
                    grad_all.at[chip],
                    6,
                    {"grp": g, "mem": to * 2 + core},
                )

            return carry

        lax.fori_loop(0, spots_in * groups, send_grad, 0)

    chunks = item_tiles // wide
    do_chunk(0, True)
    wait_for(resid_all.at[pl.ds(0, chips - 1), 0], recv_sem.at[2])
    send(resid_all.at[:, core], resid_all.at[:, core], 7, sibling)
    if chunks <= 4:
        for c in range(1, chunks):
            do_chunk(c, False)
            finish(c - 1)
    else:

        def later(c, carry):
            do_chunk(c, False)
            finish(c - 1)
            return carry

        lax.fori_loop(1, chunks, later, 0)
    finish(chunks - 1)

    loads[6].wait()
    for t in range(user_tiles):
        rows = pl.ds(t * side, side)
        user_sum[rows, :] = (
            (1.0 - prior_user) * users[rows, :].astype(f32)
            + rate_user * user_sum[rows, :]
            + noise_scale * noise[rows, :].astype(f32)
        )
    stores = [load(user_sum, new_users, 9)]
    stores[0].start()

    loads[7].wait()
    wait_for(feat_all.at[pl.ds(0, chips - 1)], recv_sem.at[4])
    wait_for(resid_all.at[:, other], recv_sem.at[7])
    link_sum = lax.dot_general(
        feat_all[...].reshape(n * owned, link_rows),
        resid_all[...].reshape(n * owned, rank),
        (((0,), (0,)), ((), ())),
        preferred_element_type=f32,
    )
    old_link = weights[pl.ds(pl.multiple_of(me * link_rows, link_rows), link_rows), :].astype(f32)
    link_out[...] = (
        (1.0 - prior_link) * old_link
        + rate_link * link_sum
        + noise_scale * link_noise[...].astype(f32)
    )
    stores.append(load(link_out, new_link, 10))
    stores[1].start()

    loads[8].wait()
    grad_all[chip] = grad_send[spot, grp]
    wait_for(grad_all.at[pl.ds(0, chips - 1)], recv_sem.at[6])

    def gather(k, total):
        return total + jnp.sum(grad_all[pl.ds(k * 8, 8)].astype(f32), axis=0)

    item_sum = lax.fori_loop(0, chips // 8, gather, jnp.zeros((owned, rank), f32))
    item_out[...] = (
        own_items
        + rate_item * item_sum
        - prior_item * resid
        + noise_scale * item_noise[...].astype(f32)
    )
    stores.append(load(item_out, new_items, 11))
    stores[2].start()

    wait_for(items.at[pl.ds(0, ring - 1), 0], send_sem.at[0])
    wait_for(feat_out, send_sem.at[1])
    wait_for(resid_all.at[pl.ds(0, chips - 1), 0], send_sem.at[2])
    wait_for(items.at[:, 0], send_sem.at[3])
    wait_for(feat_all.at[pl.ds(0, chips - 1)], send_sem.at[4])
    wait_for(grad_in, send_sem.at[5])
    wait_for(grad_all.at[pl.ds(0, chips - 1)], send_sem.at[6])
    wait_for(resid_all.at[:, 0], send_sem.at[7])
    for one in stores:
        one.wait()


def place_kernel(a, b, c, x, y, z, sem):
    copies = [
        pltpu.make_async_copy(source, target, sem.at[k])
        for k, (source, target) in enumerate(((a, x), (b, y), (c, z)))
    ]
    for copy in copies:
        copy.start()
    for copy in copies:
        copy.wait()


def per_device(
    user_factors,
    item_factors,
    link_weights,
    item_feat,
    tile_values,
    tile_scale,
    tile_place,
    tile_count,
    user_noise,
    item_noise,
    link_noise,
):
    groups = lax.axis_size("grp")
    members = lax.axis_size("mem")
    n = groups * members
    slots, side, unused = tile_values.shape
    user_count, rank = user_factors.shape
    panel_rows = item_factors.shape[0]
    owned = item_feat.shape[1]
    features = item_feat.shape[2]
    link_rows = link_noise.shape[0]
    places = (user_count // side) * (panel_rows * members // side)
    numbers = jnp.arange(slots, dtype=jnp.int32)
    match = (tile_place[None, :] == jnp.arange(places, dtype=jnp.int32)[:, None]) & (
        numbers < tile_count[0]
    )[None, :]
    slot_of = jnp.max(jnp.where(match, numbers[None, :], -1), axis=1)
    feats = item_feat[0]

    smem = pl.BlockSpec(memory_space=pltpu.SMEM)
    hbm = pl.BlockSpec(memory_space=pl.ANY)
    wide_cut = link_rows % 128 == 0
    if wide_cut:
        cut = item_noise[0]
    else:
        cut = feats.reshape(owned, n, link_rows).transpose(1, 0, 2)
    operands = [
        slot_of,
        tile_scale,
        item_factors,
        cut,
        item_noise[0],
        link_noise,
        feats,
        user_factors,
        link_weights,
        tile_values,
        user_noise,
    ]
    ring = members // 2
    chips = n // 2
    item_tiles = panel_rows * members // side
    shapes = (
        jax.ShapeDtypeStruct((user_count, rank), f32),
        jax.ShapeDtypeStruct((owned, rank), f32),
        jax.ShapeDtypeStruct((link_rows, rank), f32),
    )
    outs = pl.pallas_call(
        functools.partial(kernel, groups, members, wide_cut),
        out_shape=shapes,
        in_specs=[smem, smem] + [hbm] * 9,
        out_specs=(hbm, hbm, hbm),
        scratch_shapes=[pltpu.VMEM(x.shape, bf16) for x in operands[2:]]
        + [
            pltpu.VMEM((ring, 2, panel_rows, rank), bf16),
            pltpu.VMEM((chips, owned, link_rows), bf16),
            pltpu.VMEM((chips, 2, owned, link_rows), bf16),
            pltpu.VMEM((chips, 2, owned, link_rows), bf16),
            pltpu.VMEM((chips, 2, owned, rank), bf16),
            pltpu.VMEM((ring, 2, groups, owned, rank), f32),
            pltpu.VMEM((ring, groups, owned, rank), f32),
            pltpu.VMEM((ring, groups, owned, rank), bf16),
            pltpu.VMEM((chips, owned, rank), bf16),
            pltpu.VMEM((user_count, 2 * side), bf16),
            pltpu.VMEM((user_count, rank), f32),
            pltpu.VMEM((owned, rank), f32),
            pltpu.VMEM((link_rows, rank), f32),
            pltpu.SemaphoreType.DMA((12,)),
            pltpu.SemaphoreType.DMA((8,)),
            pltpu.SemaphoreType.DMA((8,)),
            pltpu.SemaphoreType.DMA((item_tiles // 2,)),
        ],
        compiler_params=pltpu.CompilerParams(
            collective_id=0, has_side_effects=True, vmem_limit_bytes=VMEM_BYTES
        ),
    )(*operands)
    new_users, new_items, new_link = pl.pallas_call(
        place_kernel,
        out_shape=shapes,
        in_specs=[hbm] * 3,
        out_specs=(hbm, hbm, hbm),
        scratch_shapes=[pltpu.SemaphoreType.DMA((3,))],
        compiler_params=pltpu.CompilerParams(vmem_limit_bytes=VMEM_BYTES),
    )(*outs)
    return (new_users, new_items[None], new_link)


def solution(mesh):
    in_specs = (
        P(("grp", "mem"), None),
        P("mem", None),
        P(),
        P("mem", "grp", None),
        P(("grp", "mem"), None, None),
        P(("grp", "mem")),
        P(("grp", "mem")),
        P(("grp", "mem")),
        P(("grp", "mem"), None),
        P("mem", "grp", None),
        P(("grp", "mem"), None),
    )
    out_specs = (P(("grp", "mem"), None), P("mem", "grp", None), P(("grp", "mem"), None))
    return jax.shard_map(
        per_device, mesh=mesh, in_specs=in_specs, out_specs=out_specs, check_vma=False
    )
```

time: 40.7 us -> 64.1 us (1.57)
  Pallas kernels: 27.3 us -> 61.3 us
  local copies, waits for them, and re-layouts: 10.8 us -> 0 us
    pallas_call x1 -> x2, Pallas kernels: 27.3 us -> 61.3 us  [the longest x1 37.4 us: per_device(): pl.pallas_call(place_kernel, out_shape=shapes, in_specs=[hbm] * 3, out_sp...]
    unnamed x21 -> x0, local copies, waits for them, and re-layouts: 10.8 us -> none
where the time goes in v2:
time: 64.1 us; the launch traced here: 63.8 us
  Pallas kernels  61.3 us (96%)
  between operations  1.29 us (2%)
  other arithmetic  1.26 us (2%)
    pallas_call x1, Pallas kernels, per_device(): pl.pallas_call(place_kernel, out_shape=shapes, in_specs=[hbm] * 3, out_sp...  37.4 us
    pallas_call x1, Pallas kernels, per_device(): pl.pallas_call(functools.partial(kernel, groups, members, wide_cut), out_...  23.9 us

profile of v2, /device:TPU:0, one launch (start us, length us, event | category | flops | bytes accessed | tf_op | source)
XLA Modules:
  0.0 63.8 jit_solution(6116013873721668934)
XLA Ops:
  1.3 1.3 %select_reduce_fusion.slot_of = s32[32]{0:T(128)} fusion(s32[24]{0:T(128)} %param.17, pred[24]{0:T(512)(128)(4,1)S(1)} %iota_compare_fusion.1), kind=kLoop, calls=%fused_computation | loop fusion | flops 3040 | bytes 248 | tf_op jit(solution)/shard_map/reduce_max | solution.py:366
  2.5 23.9 %shard_map.130 = (f32[1024,256]{1,0:T(8,128)}, f32[16,256]{1,0:T(8,128)}, f32[128,256]{1,0:T(8,128)}) custom-call(s32[32]{0:T(128)} %select_reduce_fusion.slot_of, f32[24]{0:T(128)} %scales.1, bf16[32,256]{1,0:T(8,128)(2,1)} %panel_hbm.1, bf16[16,256]{1,0:T(8,128)(2,1)} %bitcast.6, bf16[16,256]{1,0:T(8,128)(2,1)} %bitcast.7, ...), custom_call_target="tpu_custom_call" | custom-call | tf_op jit(solution)/shard_map/pallas_call | solution.py:397
  26.5 37.4 %shard_map.131 = (f32[1024,256]{1,0:T(8,128)}, f32[16,256]{1,0:T(8,128)}, f32[128,256]{1,0:T(8,128)}) custom-call(f32[1024,256]{1,0:T(8,128)} %get-tuple-element.9.a, f32[16,256]{1,0:T(8,128)} %get-tuple-element.10.b, f32[128,256]{1,0:T(8,128)} %get-tuple-element.11.c), custom_call_target="tpu_custom_call" | custom-call | tf_op jit(solution)/shard_map/pallas_call | solution.py:426
  (1 shorter events, 0.0 us)

commit v3 on v2

--- a/solution.py
+++ b/solution.py
@@ -25,7 +25,8 @@
     groups,
     members,
     wide_cut,
-    slot_of,
+    slot_place,
+    live_slots,
     scales,
     panel_hbm,
     cut_hbm,
@@ -61,6 +62,7 @@
     user_sum,
     item_out,
     link_out,
+    slot_of,
     local_sem,
     send_sem,
     recv_sem,
@@ -127,6 +129,28 @@
         return carry
 
     lax.fori_loop(1, chips, greet, 0)
+
+    slots = tiles.shape[0]
+    step = 8 if slots % 8 == 0 else 1
+    live_count = live_slots[0]
+
+    def find(q, carry):
+        def look(k, best):
+            for j in range(step):
+                at = k * step + j
+                best = jnp.where((slot_place[at] == q) & (at < live_count), at, best)
+            return best
+
+        best = jnp.int32(-1)
+        if slots <= 32:
+            for k in range(slots // step):
+                best = look(k, best)
+        else:
+            best = lax.fori_loop(0, slots // step, look, best)
+        slot_of[q] = best
+        return carry
+
+    lax.fori_loop(0, user_tiles * item_tiles, find, 0)
 
     loads[0].wait()
     items[spot, core] = panel[...]
@@ -325,14 +349,27 @@
         one.wait()
 
 
-def place_kernel(a, b, c, x, y, z, sem):
-    copies = [
-        pltpu.make_async_copy(source, target, sem.at[k])
-        for k, (source, target) in enumerate(((a, x), (b, y), (c, z)))
+def place_kernel(a, b, c, x, y, z, held_a, held_b, held_c, in_sem, out_sem):
+    pieces = 8
+    rows = a.shape[0] // pieces
+    paths = [(b, held_b, y), (c, held_c, z)]
+    for k in range(pieces):
+        part = pl.ds(k * rows, rows)
+        paths.append((a.at[part], held_a.at[part], x.at[part]))
+    ins = [
+        pltpu.make_async_copy(source, held, in_sem.at[k])
+        for k, (source, held, target) in enumerate(paths)
     ]
-    for copy in copies:
+    outs = [
+        pltpu.make_async_copy(held, target, out_sem.at[k])
+        for k, (source, held, target) in enumerate(paths)
+    ]
+    for copy in ins:
         copy.start()
-    for copy in copies:
+    for first, second in zip(ins, outs):
+        first.wait()
+        second.start()
+    for copy in outs:
         copy.wait()
 
 
@@ -359,11 +396,6 @@
     features = item_feat.shape[2]
     link_rows = link_noise.shape[0]
     places = (user_count // side) * (panel_rows * members // side)
-    numbers = jnp.arange(slots, dtype=jnp.int32)
-    match = (tile_place[None, :] == jnp.arange(places, dtype=jnp.int32)[:, None]) & (
-        numbers < tile_count[0]
-    )[None, :]
-    slot_of = jnp.max(jnp.where(match, numbers[None, :], -1), axis=1)
     feats = item_feat[0]
 
     smem = pl.BlockSpec(memory_space=pltpu.SMEM)
@@ -374,7 +406,8 @@
     else:
         cut = feats.reshape(owned, n, link_rows).transpose(1, 0, 2)
     operands = [
-        slot_of,
+        tile_place,
+        tile_count,
         tile_scale,
         item_factors,
         cut,
@@ -397,9 +430,9 @@
     outs = pl.pallas_call(
         functools.partial(kernel, groups, members, wide_cut),
         out_shape=shapes,
-        in_specs=[smem, smem] + [hbm] * 9,
+        in_specs=[smem, smem, smem] + [hbm] * 9,
         out_specs=(hbm, hbm, hbm),
-        scratch_shapes=[pltpu.VMEM(x.shape, bf16) for x in operands[2:]]
+        scratch_shapes=[pltpu.VMEM(x.shape, bf16) for x in operands[3:]]
         + [
             pltpu.VMEM((ring, 2, panel_rows, rank), bf16),
             pltpu.VMEM((chips, owned, link_rows), bf16),
@@ -414,6 +447,7 @@
             pltpu.VMEM((user_count, rank), f32),
             pltpu.VMEM((owned, rank), f32),
             pltpu.VMEM((link_rows, rank), f32),
+            pltpu.SMEM((places,), jnp.int32),
             pltpu.SemaphoreType.DMA((12,)),
             pltpu.SemaphoreType.DMA((8,)),
             pltpu.SemaphoreType.DMA((8,)),
@@ -428,7 +462,8 @@
         out_shape=shapes,
         in_specs=[hbm] * 3,
         out_specs=(hbm, hbm, hbm),
-        scratch_shapes=[pltpu.SemaphoreType.DMA((3,))],
+        scratch_shapes=[pltpu.VMEM(x.shape, f32) for x in shapes]
+        + [pltpu.SemaphoreType.DMA((10,)), pltpu.SemaphoreType.DMA((10,))],
         compiler_params=pltpu.CompilerParams(vmem_limit_bytes=VMEM_BYTES),
     )(*outs)
     return (new_users, new_items[None], new_link)

time: 64.1 us -> 27.8 us (0.43)
  Pallas kernels: 61.3 us -> 26.2 us
  other arithmetic: 1.26 us -> 0 us
    pallas_call x1, Pallas kernels: 37.4 us -> 2.18 us  [per_device(): pl.pallas_call(place_kernel, out_shape=shapes, in_specs=[hbm] * 3, out_sp...]
    reduce_max x1 -> x0, other arithmetic: 1.26 us -> none  [per_device(): slot_of = jnp.max(jnp.where(match, numbers[None, :], -1), axis=1)]
where the time goes in v3:
time: 27.8 us; the launch traced here: 27.5 us
  Pallas kernels  26.2 us (94%)
  between operations  1.29 us (5%)
    pallas_call x1, Pallas kernels, per_device(): pl.pallas_call(functools.partial(kernel, groups, members, wide_cut), out_...  24.1 us
    pallas_call x1, Pallas kernels, per_device(): pl.pallas_call(place_kernel, out_shape=shapes, in_specs=[hbm] * 3, out_sp...  2.18 us

profile of v3, /device:TPU:0, one launch (start us, length us, event | category | flops | bytes accessed | tf_op | source)
XLA Modules:
  0.0 27.5 jit_solution(10205542449464910685)
XLA Ops:
  1.3 24.1 %shard_map.130 = (f32[1024,256]{1,0:T(8,128)}, f32[16,256]{1,0:T(8,128)}, f32[128,256]{1,0:T(8,128)}) custom-call(s32[24]{0:T(128)} %slot_place.1, s32[1]{0:T(128)S(6)} %copy.14.live_slots, f32[24]{0:T(128)} %scales.1, bf16[32,256]{1,0:T(8,128)(2,1)} %panel_hbm.1, bf16[16,256]{1,0:T(8,128)(2,1)} %bitcast.4, bf16[16,256]{1,0:T(8,128)(2,1)} %bitcast.5, ...), custom_call_target="tpu_custom_call" | custom-call | tf_op jit(solution)/shard_map/pallas_call | solution.py:430
  25.4 2.2 %shard_map.131 = (f32[1024,256]{1,0:T(8,128)}, f32[16,256]{1,0:T(8,128)}, f32[128,256]{1,0:T(8,128)}) custom-call(f32[1024,256]{1,0:T(8,128)} %get-tuple-element.9.a, f32[16,256]{1,0:T(8,128)} %get-tuple-element.10.b, f32[128,256]{1,0:T(8,128)} %get-tuple-element.11.c), custom_call_target="tpu_custom_call" | custom-call | tf_op jit(solution)/shard_map/pallas_call | solution.py:460

commit v4 on v3

--- a/solution.py
+++ b/solution.py
@@ -289,7 +289,6 @@
             return carry
 
         lax.fori_loop(1, chunks, later, 0)
-    finish(chunks - 1)
 
     loads[6].wait()
     for t in range(user_tiles):
@@ -301,6 +300,7 @@
         )
     stores = [load(user_sum, new_users, 9)]
     stores[0].start()
+    finish(chunks - 1)
 
     loads[7].wait()
     wait_for(feat_all.at[pl.ds(0, chips - 1)], recv_sem.at[4])

time: 27.8 us -> 27.8 us (level)
  no operation moved by 1% of the time
where the time goes in v4:
time: 27.8 us; the launch traced here: 27.5 us
  Pallas kernels  26.2 us (94%)
  between operations  1.29 us (5%)
    pallas_call x1, Pallas kernels, per_device(): pl.pallas_call(functools.partial(kernel, groups, members, wide_cut), out_...  24.1 us
    pallas_call x1, Pallas kernels, per_device(): pl.pallas_call(place_kernel, out_shape=shapes, in_specs=[hbm] * 3, out_sp...  2.18 us

profile of v4, /device:TPU:0, one launch (start us, length us, event | category | flops | bytes accessed | tf_op | source)
XLA Modules:
  0.0 27.5 jit_solution(6155776268037173031)
XLA Ops:
  1.3 24.1 %shard_map.130 = (f32[1024,256]{1,0:T(8,128)}, f32[16,256]{1,0:T(8,128)}, f32[128,256]{1,0:T(8,128)}) custom-call(s32[24]{0:T(128)} %slot_place.1, s32[1]{0:T(128)S(6)} %copy.14.live_slots, f32[24]{0:T(128)} %scales.1, bf16[32,256]{1,0:T(8,128)(2,1)} %panel_hbm.1, bf16[16,256]{1,0:T(8,128)(2,1)} %bitcast.4, bf16[16,256]{1,0:T(8,128)(2,1)} %bitcast.5, ...), custom_call_target="tpu_custom_call" | custom-call | tf_op jit(solution)/shard_map/pallas_call | solution.py:430
  25.4 2.2 %shard_map.131 = (f32[1024,256]{1,0:T(8,128)}, f32[16,256]{1,0:T(8,128)}, f32[128,256]{1,0:T(8,128)}) custom-call(f32[1024,256]{1,0:T(8,128)} %get-tuple-element.9.a, f32[16,256]{1,0:T(8,128)} %get-tuple-element.10.b, f32[128,256]{1,0:T(8,128)} %get-tuple-element.11.c), custom_call_target="tpu_custom_call" | custom-call | tf_op jit(solution)/shard_map/pallas_call | solution.py:460

commit v5 on v4

--- a/solution.py
+++ b/solution.py
@@ -185,15 +185,15 @@
     resid = own_items - jnp.dot(feats[...], weights[...], preferred_element_type=f32)
     resid_all[chip, core] = resid.astype(bf16)
 
+    wait_for(items.at[pl.ds(0, ring - 1), 0], recv_sem.at[0])
+    send(items.at[:, core], items.at[:, core], 3, sibling)
+
     def send_resid(k, carry):
         q = lax.rem(chip + k, chips)
         send(resid_all.at[chip, core], resid_all.at[chip, core], 2, mate(q))
         return carry
 
     lax.fori_loop(1, chips, send_resid, 0)
-
-    wait_for(items.at[pl.ds(0, ring - 1), 0], recv_sem.at[0])
-    send(items.at[:, core], items.at[:, core], 3, sibling)
 
     wait_for(feat_out, recv_sem.at[1])
     feat_all[chip] = feat_pair[chip]

time: 27.8 us -> 28.2 us (1.014)
  Pallas kernels: 26.2 us -> 26.6 us
    pallas_call x1, Pallas kernels: 24.1 us -> 24.5 us  [per_device(): pl.pallas_call(functools.partial(kernel, groups, members, wide_cut), out_...]
where the time goes in v5:
time: 28.2 us; the launch traced here: 27.9 us
  Pallas kernels  26.6 us (94%)
  between operations  1.29 us (5%)
    pallas_call x1, Pallas kernels, per_device(): pl.pallas_call(functools.partial(kernel, groups, members, wide_cut), out_...  24.5 us
    pallas_call x1, Pallas kernels, per_device(): pl.pallas_call(place_kernel, out_shape=shapes, in_specs=[hbm] * 3, out_sp...  2.18 us

profile of v5, /device:TPU:0, one launch (start us, length us, event | category | flops | bytes accessed | tf_op | source)
XLA Modules:
  0.0 27.9 jit_solution(15123595338304766659)
XLA Ops:
  1.3 24.5 %shard_map.130 = (f32[1024,256]{1,0:T(8,128)}, f32[16,256]{1,0:T(8,128)}, f32[128,256]{1,0:T(8,128)}) custom-call(s32[24]{0:T(128)} %slot_place.1, s32[1]{0:T(128)S(6)} %copy.14.live_slots, f32[24]{0:T(128)} %scales.1, bf16[32,256]{1,0:T(8,128)(2,1)} %panel_hbm.1, bf16[16,256]{1,0:T(8,128)(2,1)} %bitcast.4, bf16[16,256]{1,0:T(8,128)(2,1)} %bitcast.5, ...), custom_call_target="tpu_custom_call" | custom-call | tf_op jit(solution)/shard_map/pallas_call | solution.py:430
  25.8 2.2 %shard_map.131 = (f32[1024,256]{1,0:T(8,128)}, f32[16,256]{1,0:T(8,128)}, f32[128,256]{1,0:T(8,128)}) custom-call(f32[1024,256]{1,0:T(8,128)} %get-tuple-element.9.a, f32[16,256]{1,0:T(8,128)} %get-tuple-element.10.b, f32[128,256]{1,0:T(8,128)} %get-tuple-element.11.c), custom_call_target="tpu_custom_call" | custom-call | tf_op jit(solution)/shard_map/pallas_call | solution.py:460

commit v6 on v5

--- a/solution.py
+++ b/solution.py
@@ -185,9 +185,6 @@
     resid = own_items - jnp.dot(feats[...], weights[...], preferred_element_type=f32)
     resid_all[chip, core] = resid.astype(bf16)
 
-    wait_for(items.at[pl.ds(0, ring - 1), 0], recv_sem.at[0])
-    send(items.at[:, core], items.at[:, core], 3, sibling)
-
     def send_resid(k, carry):
         q = lax.rem(chip + k, chips)
         send(resid_all.at[chip, core], resid_all.at[chip, core], 2, mate(q))
@@ -204,6 +201,9 @@
         return carry
 
     lax.fori_loop(1, chips, send_feat, 0)
+
+    wait_for(items.at[pl.ds(0, ring - 1), 0], recv_sem.at[0])
+    send(items.at[:, core], items.at[:, core], 3, sibling)
 
     loads[4].wait()
     loads[5].wait()

time: 28.2 us -> 27.9 us (0.989)
  Pallas kernels: 26.6 us -> 26.3 us
    pallas_call x1, Pallas kernels: 24.5 us -> 24.2 us  [per_device(): pl.pallas_call(functools.partial(kernel, groups, members, wide_cut), out_...]
where the time goes in v6:
time: 27.9 us; the launch traced here: 27.6 us
  Pallas kernels  26.3 us (94%)
  between operations  1.29 us (5%)
    pallas_call x1, Pallas kernels, per_device(): pl.pallas_call(functools.partial(kernel, groups, members, wide_cut), out_...  24.2 us
    pallas_call x1, Pallas kernels, per_device(): pl.pallas_call(place_kernel, out_shape=shapes, in_specs=[hbm] * 3, out_sp...  2.18 us

profile of v6, /device:TPU:0, one launch (start us, length us, event | category | flops | bytes accessed | tf_op | source)
XLA Modules:
  0.0 27.6 jit_solution(17770281508040257376)
XLA Ops:
  1.3 24.2 %shard_map.130 = (f32[1024,256]{1,0:T(8,128)}, f32[16,256]{1,0:T(8,128)}, f32[128,256]{1,0:T(8,128)}) custom-call(s32[24]{0:T(128)} %slot_place.1, s32[1]{0:T(128)S(6)} %copy.14.live_slots, f32[24]{0:T(128)} %scales.1, bf16[32,256]{1,0:T(8,128)(2,1)} %panel_hbm.1, bf16[16,256]{1,0:T(8,128)(2,1)} %bitcast.4, bf16[16,256]{1,0:T(8,128)(2,1)} %bitcast.5, ...), custom_call_target="tpu_custom_call" | custom-call | tf_op jit(solution)/shard_map/pallas_call | solution.py:430
  25.5 2.2 %shard_map.131 = (f32[1024,256]{1,0:T(8,128)}, f32[16,256]{1,0:T(8,128)}, f32[128,256]{1,0:T(8,128)}) custom-call(f32[1024,256]{1,0:T(8,128)} %get-tuple-element.9.a, f32[16,256]{1,0:T(8,128)} %get-tuple-element.10.b, f32[128,256]{1,0:T(8,128)} %get-tuple-element.11.c), custom_call_target="tpu_custom_call" | custom-call | tf_op jit(solution)/shard_map/pallas_call | solution.py:460
